TPU v7x, 32 devices: a whole 2x2x4 slice. The times are simulated.
32 devices in a mesh: group: 2 (over x), expert: 16 (over z, y, core).
Axes of the slice: x: 2, y: 2, z: 4, core: 2. Of those that a mesh axis runs over, the one named last changes fastest.
Arguments:
- resid: bfloat16 [2048, 4096], P(('group', 'expert')), parts along dimension 0, may hold values from -30 to 30
- queries: bfloat16 [2048, 4096], P(('group', 'expert')), parts along dimension 0, may hold values from -8 to 8
- block_keys: bfloat16 [2048, 512], P(('group', 'expert')), parts along dimension 0, may hold values from -6 to 6
- block_values: bfloat16 [2048, 512], P(('group', 'expert')), parts along dimension 0, may hold values from -6 to 6
- cache_keys: bfloat16 [64, 1024, 512], P(('group', 'expert')), parts along dimension 0, may hold values from -8 to 8
- cache_values: bfloat16 [64, 1024, 512], P(('group', 'expert')), parts along dimension 0, may hold values from -6 to 6
- prefix_len: int32 [64], P(('group', 'expert')), parts along dimension 0, may hold values from 2 to 1024
- norm_gain: float32 [4096], replicated, may hold values from 0.5 to 1.5
- expert_ids: int32 [2048, 4], P(('group', 'expert')), parts along dimension 0, may hold values from 0 to 7, all different within a row; in each aligned block of 64 rows (0 to 63, 64 to 127, ...) at most 48 rows name the same one
- route_weights: float32 [2048, 4], P(('group', 'expert')), parts along dimension 0, may hold values from 0.1 to 1
- w_gate: bfloat16 [16, 4096, 256], P('expert'), may hold values from -0.09375 to 0.09375
- w_up: bfloat16 [16, 4096, 256], P('expert'), may hold values from -0.09375 to 0.09375
- w_down: bfloat16 [16, 256, 4096], P('expert'), may hold values from -0.25 to 0.25
Outputs:
- layer_out: bfloat16 [2048, 4096], P(('group', 'expert')), parts along dimension 0
There are 2 independent parts, one for each index of `group`. A program takes and returns all parts, laid end to end along the dimension named above; an argument that names none is the same for every part. Nothing has to cross between parts.
Inputs may be any that keep to these rules, and one draw needn't show every extreme that they name: `expert_ids`: each row names 4 different experts; in each aligned block of 64 rows (the rows of one device) no expert is named by more than 48 rows, a bound that some block reaches.
All inputs are finite; a program needn't handle non-finite values.
Results may differ from a plain program's by a relative error of at most 0.008.
Values may be sent and summed in bfloat16 or wider, within the bound.
No kernel may reach another device: no remote copies, remote signals or barrier semaphores. Data moves between devices by JAX's collectives and lax.ppermute only.
A program may use at most 128 MiB of HBM per device.

v0:
```python
import jax
import jax.numpy as jnp
from jax import lax
from jax.sharding import PartitionSpec as P

HEADS = 32
KV_HEADS = 4
HEAD_DIM = 128
BLOCK = 32


def attend_request(query_rows, own_keys, own_values, cached_keys, cached_values, prefix_length):
    groups = HEADS // KV_HEADS
    prefix = cached_keys.shape[0]
    block = query_rows.shape[0]
    query_heads = query_rows.reshape(block, KV_HEADS, groups, HEAD_DIM)
    key_rows = jnp.concatenate([cached_keys, own_keys], 0).reshape(-1, KV_HEADS, HEAD_DIM)
    value_rows = jnp.concatenate([cached_values, own_values], 0).reshape(-1, KV_HEADS, HEAD_DIM)
    scores = jnp.einsum(
        "ikgd,jkd->kgij", query_heads, key_rows, preferred_element_type=jnp.float32
    ) * HEAD_DIM ** (-0.5)
    position = jnp.arange(prefix + block, dtype=jnp.int32)
    usable = (position < prefix_length) | (position >= prefix)
    scores = jnp.where(usable, scores, jnp.float32(-1e30))
    top_score = jnp.max(scores, -1, keepdims=True)
    weights = jnp.exp(scores - top_score)
    probs = (weights / jnp.sum(weights, -1, keepdims=True)).astype(jnp.bfloat16)
    mixed = jnp.einsum("kgij,jkd->ikgd", probs, value_rows, preferred_element_type=jnp.float32)
    return mixed.reshape(block, HEADS * HEAD_DIM).astype(jnp.bfloat16)


def local(
    resid,
    queries,
    block_keys,
    block_values,
    cache_keys,
    cache_values,
    prefix_len,
    norm_gain,
    expert_ids,
    route_weights,
    w_gate,
    w_up,
    w_down,
):
    requests = cache_keys.shape[0]
    width = resid.shape[1]
    attended = jax.vmap(attend_request)(
        queries.reshape(requests, BLOCK, -1),
        block_keys.reshape(requests, BLOCK, -1),
        block_values.reshape(requests, BLOCK, -1),
        cache_keys,
        cache_values,
        prefix_len,
    ).reshape(-1, width)
    hidden = (resid.astype(jnp.float32) + attended.astype(jnp.float32)).astype(jnp.bfloat16)
    hidden_wide = hidden.astype(jnp.float32)
    normed = (
        hidden_wide
        * lax.rsqrt(jnp.mean(hidden_wide * hidden_wide, -1, keepdims=True) + 1e-06)
        * norm_gain
    ).astype(jnp.bfloat16)
    devices = lax.axis_size("expert")
    experts = devices // 2
    tokens, topk = expert_ids.shape
    capacity = 2 * ((3 * tokens * topk + 4 * experts - 1) // (4 * experts))
    flat_ids = expert_ids.reshape(-1)
    onehot = (flat_ids[:, None] == jnp.arange(experts, dtype=jnp.int32)[None, :]).astype(jnp.int32)
    earlier = jnp.cumsum(onehot, 0) - onehot
    slot_rank = jnp.sum(earlier * onehot, 1)
    target = flat_ids * capacity + slot_rank
    token_of = jnp.arange(tokens * topk, dtype=jnp.int32) // topk
    outgoing = jnp.zeros((experts * capacity, width), jnp.bfloat16).at[target].set(normed[token_of])
    doubled = jnp.repeat(outgoing.reshape(experts, capacity, width), 2, axis=0)
    arrived = lax.all_to_all(doubled, "expert", split_axis=0, concat_axis=0, tiled=True)
    sources = arrived.shape[0]
    items = arrived.shape[1]
    flat_rows = arrived.reshape(-1, width)
    gate_out = jnp.dot(flat_rows, w_gate[0], preferred_element_type=jnp.float32)
    upward = jnp.dot(flat_rows, w_up[0], preferred_element_type=jnp.float32)
    active = (jax.nn.silu(gate_out) * upward).astype(jnp.bfloat16)
    partial_value = jnp.dot(active, w_down[0], preferred_element_type=jnp.float32).astype(
        jnp.bfloat16
    )
    returned = lax.all_to_all(
        partial_value.reshape(sources, items, width),
        "expert",
        split_axis=0,
        concat_axis=0,
        tiled=True,
    )
    paired = returned.reshape(experts, 2, capacity, width)
    expert_out = (paired[:, 0].astype(jnp.float32) + paired[:, 1].astype(jnp.float32)).astype(
        jnp.bfloat16
    )
    flat_out = expert_out.reshape(-1, width)
    weighted = flat_out[target].astype(jnp.float32) * route_weights.reshape(-1)[:, None]
    mixture = jnp.sum(weighted.reshape(tokens, topk, width), 1)
    return (hidden_wide + mixture).astype(jnp.bfloat16)


def solution(mesh):
    placed = (
        P(("group", "expert"), None),
        P(("group", "expert"), None),
        P(("group", "expert"), None),
        P(("group", "expert"), None),
        P(("group", "expert"), None, None),
        P(("group", "expert"), None, None),
        P(("group", "expert")),
        P(),
        P(("group", "expert"), None),
        P(("group", "expert"), None),
        P("expert", None, None),
        P("expert", None, None),
        P("expert", None, None),
    )
    return jax.shard_map(
        local, mesh=mesh, in_specs=placed, out_specs=P(("group", "expert"), None), check_vma=False
    )
```

profile of v0, /device:TPU:13, one launch (start us, length us, event | category | flops | bytes accessed | tf_op | source)
XLA Modules:
  0.0 379.9 jit_solution(14057844381983226956)
XLA Ops:
  0.0 0.0 copy-start
  0.0 0.9 copy.27
  0.9 0.1 eq.29
  1.0 0.1 eq.25
  1.1 0.7 broadcast_multiply_fusion
  1.8 4.0 %copy.21 = bf16[2,1024,512]{1,2,0:T(8,128)(2,1)} copy(bf16[2,1024,512]{2,1,0:T(8,128)(2,1)} %param.17) | data formatting | bytes 4194304 | tf_op args[4]
  5.8 4.0 %copy.22 = bf16[2,1024,4,128]{3,1,2,0:T(8,128)(2,1)} copy(bf16[2,1024,4,128]{1,3,2,0:T(8,128)(2,1)} %bitcast.81) | data formatting | bytes 4194304 | tf_op jit(solution)/shard_map/vmap()/concatenate | solution.py:17
  9.8 0.0 copy-done.3
  9.8 0.1 copy.36
  9.9 0.0 copy-done.4
  10.0 4.0 %copy.18 = bf16[2,1024,512]{1,2,0:T(8,128)(2,1)} copy(bf16[2,1024,512]{2,1,0:T(8,128)(2,1)} %param.18) | data formatting | bytes 4194304 | tf_op args[5]
  13.9 4.0 %copy.19 = bf16[2,1024,4,128]{3,1,2,0:T(8,128)(2,1)} copy(bf16[2,1024,4,128]{1,3,2,0:T(8,128)(2,1)} %bitcast.82) | data formatting | bytes 4194304 | tf_op jit(solution)/shard_map/vmap()/concatenate | solution.py:18
  17.9 0.0 copy-done.5
  18.0 0.0 copy-done.8
  18.0 0.1 compare_or_fusion
  18.1 3.0 fusion.11
  21.0 0.0 copy-start.2
  21.1 5.5 %fusion.52 = (f32[2,4,8,32]{3,2,1,0:T(8,128)S(1)}, f32[2,4,8,32,1056]{4,3,2,1,0:T(8,128)}) fusion(f32[2,4,1056,32,8]{2,3,4,1,0:T(8,128)S(1)} %fusion.11, pred[2,1056]{1,0:T(4,128)(4,1)S(1)} %compare_or_fusion), kind=kOutput, calls=%fused_computation.78 | output fusion | flops 12977183 | bytes 17311808 | tf_op jit(solution)/shard_map/vmap()/sub | solution.py:26
  26.5 0.0 copy-done.2
  26.5 4.7 %fusion.24 = f32[2,32,4,8,128]{4,1,3,2,0:T(8,128)S(1)} fusion(f32[2,4,8,32,1056]{4,3,2,1,0:T(8,128)} %get-tuple-element.8, f32[2,4,8,32]{3,2,1,0:T(8,128)S(1)} %get-tuple-element.7, bf16[2,32,4,128]{3,1,2,0:T(8,128)(2,1)S(1)} %copy.20, bf16[2,1024,4,128]{3,1,2,0:T(8,128)(2,1)S(1)} %copy-done.2), kind=kOutput, calls=%fused_computation.39 | convolution fusion | flops 562823168 | bytes 11870208 | tf_op jit(solution)/shard_map/vmap(kgij,jkd->ikgd)/dot_general | solution.py:28
  31.2 0.0 copy-start.6
  31.2 0.6 copy.25
  31.8 1.2 reshape.159
  33.0 1.6 fusion.33
  34.6 0.7 reduce-window.6
  35.4 0.2 slice_reduce_fusion
  35.6 0.1 copy.26
  35.7 0.1 mul.65
  35.9 0.1 fusion.45
  36.0 0.0 copy-done.6
  36.0 0.2 fusion.35
  36.2 11.6 %scatter_custom_fusion = bf16[384,4096]{1,0:T(8,128)(2,1)} fusion(s32[256]{0:T(256)S(1)} %bitcast.88, bf16[64,4096]{1,0:T(8,128)(2,1)S(1)} %fusion.35, s32[1024]{0:T(1024)S(1)} %pad_clamp_fusion.1, bf16[]{:T(256)} %constant.38.clone.1), kind=kCustom, calls=%fused_computation.31 | custom fusion | bytes 3145730 | tf_op jit(solution)/shard_map/scatter | solution.py:74
  47.8 2.8 broadcast_in_dim.15
  50.5 0.0 copy-start.9
  50.6 143.7 %all_to_all.10 = bf16[16,48,4096]{2,1,0:T(8,128)(2,1)S(1)} all-to-all(bf16[16,48,4096]{2,1,0:T(8,128)(2,1)S(1)} %bitcast.79), channel_id=1, replica_groups=mesh['group'=2,'expert'=16] {'expert'}, dimensions={0} | all-to-all | bytes 12582912 | tf_op jit(solution)/shard_map/all_to_all | solution.py:76
  194.2 2.7 copy-done.1
  196.9 0.0 copy-done.9
  196.9 2.7 fusion.17
  199.6 0.0 copy-done
  199.6 12.8 %convolution_convert_fusion = bf16[768,4096]{1,0:T(8,128)(2,1)} fusion(bf16[1,256,4096]{2,1,0:T(8,128)(2,1)S(1)} %copy-done, bf16[768,4096]{1,0:T(8,128)(2,1)} %bitcast.85, bf16[1,4096,256]{2,1,0:T(8,128)(2,1)} %param.24, f32[768,256]{1,0:T(8,128)} %fusion.17), kind=kOutput, calls=%fused_computation.10 | convolution fusion | flops 3225550848 | bytes 17563648 | tf_op jit(solution)/shard_map/dot_general | solution.py:83
  212.4 5.6 %all-to-all-start.1 = ((bf16[16,48,4096]{2,1,0:T(8,128)(2,1)}), bf16[16,48,4096]{2,1,0:T(8,128)(2,1)}, u32[]{:S(2)}, u32[]{:S(2)}) async-start(bf16[16,48,4096]{2,1,0:T(8,128)(2,1)} %bitcast.83), calls=%async_computation.1 | async-start | bytes 12582912 | tf_op jit(solution)/shard_map/all_to_all | solution.py:86
  218.0 0.1 copy.31
  218.1 137.3 %all-to-all-done.1 = bf16[16,48,4096]{2,1,0:T(8,128)(2,1)} async-done(((bf16[16,48,4096]{2,1,0:T(8,128)(2,1)}), bf16[16,48,4096]{2,1,0:T(8,128)(2,1)}, u32[]{:S(2)}, u32[]{:S(2)}) %all-to-all-start.1) | async-done | bytes 6291488 | tf_op jit(solution)/shard_map/all_to_all | solution.py:86
  355.4 5.8 %add_convert_fusion = bf16[8,1,48,4096]{3,2,0,1:T(8,128)(2,1)} fusion(bf16[8,2,48,4096]{3,2,1,0:T(8,128)(2,1)} %bitcast.20), kind=kLoop, calls=%fused_computation.11 | loop fusion | flops 6291456 | bytes 9437184 | tf_op jit(solution)/shard_map/convert_element_type | solution.py:94
  361.3 7.5 %gather_fusion = bf16[256,4096]{1,0:T(8,128)(2,1)} fusion(bf16[384,4096]{1,0:T(8,128)(2,1)} %bitcast.78, s32[1024]{0:T(1024)S(1)} %pad_clamp_fusion), kind=kCustom, calls=%fused_computation.1 | custom fusion | bytes 4195328 | tf_op jit(solution)/shard_map/gather | solution.py:98
  368.8 4.7 %reshape.160 = f32[64,4,4096]{2,1,0:T(4,128)} reshape(bf16[256,4096]{1,0:T(8,128)(2,1)} %gather_fusion) | data formatting | bytes 6291456 | tf_op jit(solution)/shard_map/convert_element_type | solution.py:98
  373.5 5.4 %multiply_reduce_fusion = f32[64,4096]{1,0:T(8,128)S(1)} fusion(f32[64,4,4096]{2,1,0:T(4,128)} %reshape.160, f32[64,4]{1,0:T(8,128)S(1)} %copy.31), kind=kLoop, calls=%fused_computation.16 | loop fusion | flops 1835008 | bytes 5243904 | tf_op jit(solution)/shard_map/reduce_sum | solution.py:99
  378.9 0.9 fusion.36
  (20 shorter events, 0.2 us)
Async XLA Ops:
  0.0 199.6 %copy-start = (bf16[1,256,4096]{2,1,0:T(8,128)(2,1)S(1)}, bf16[1,256,4096]{2,1,0:T(8,128)(2,1)}, u32[]{:S(2)}) copy-start(bf16[1,256,4096]{2,1,0:T(8,128)(2,1)} %param.25) | copy-start | bytes 6291460
  5.8 4.0 %copy-start.3 = (bf16[64,4096]{1,0:T(8,128)(2,1)S(1)}, bf16[64,4096]{1,0:T(8,128)(2,1)}, u32[]{:S(2)}) copy-start(bf16[64,4096]{1,0:T(8,128)(2,1)} %param.14) | copy-start | bytes 1572868
  5.8 4.1 %copy-start.4 = (bf16[64,512]{1,0:T(8,128)(2,1)S(1)}, bf16[64,512]{1,0:T(8,128)(2,1)}, u32[]{:S(2)}) copy-start(bf16[64,512]{1,0:T(8,128)(2,1)} %param.15) | copy-start | bytes 196612
  13.9 4.0 %copy-start.5 = (bf16[64,512]{1,0:T(8,128)(2,1)S(1)}, bf16[64,512]{1,0:T(8,128)(2,1)}, u32[]{:S(2)}) copy-start(bf16[64,512]{1,0:T(8,128)(2,1)} %param.16) | copy-start | bytes 196612
  13.9 4.0 %copy-start.8 = (s32[2]{0:T(128)S(1)}, s32[2]{0:T(128)}, u32[]{:S(2)}) copy-start(s32[2]{0:T(128)} %param.19) | copy-start | bytes 28
  21.0 5.5 %copy-start.2 = (bf16[2,1024,4,128]{3,1,2,0:T(8,128)(2,1)S(1)}, bf16[2,1024,4,128]{3,1,2,0:T(8,128)(2,1)}, u32[]{:S(2)}) copy-start(bf16[2,1024,4,128]{3,1,2,0:T(8,128)(2,1)} %copy.19) | copy-start | bytes 6291460
  31.2 4.8 %copy-start.6 = (f32[4096]{0:T(1024)S(1)}, f32[4096]{0:T(1024)}, u32[]{:S(2)}) copy-start(f32[4096]{0:T(1024)} %param.20) | copy-start | bytes 49156
  50.5 146.3 %copy-start.9 = (bf16[1,4096,256]{2,1,0:T(8,128)(2,1)S(1)}, bf16[1,4096,256]{2,1,0:T(8,128)(2,1)}, u32[]{:S(2)}) copy-start(bf16[1,4096,256]{2,1,0:T(8,128)(2,1)} %param.23) | copy-start | bytes 6291460
  194.2 2.7 copy-start.1
  212.4 5.6 %copy-start.7 = (f32[64,4]{0,1:T(4,128)S(1)}, f32[64,4]{0,1:T(4,128)}, u32[]{:S(2)}) copy-start(f32[64,4]{0,1:T(4,128)} %param.22) | copy-start | bytes 3076
  212.4 143.0 %all-to-all-start.1 = ((bf16[16,48,4096]{2,1,0:T(8,128)(2,1)}), bf16[16,48,4096]{2,1,0:T(8,128)(2,1)}, u32[]{:S(2)}, u32[]{:S(2)}) async-start(bf16[16,48,4096]{2,1,0:T(8,128)(2,1)} %bitcast.83), calls=%async_computation.1 | async-start | bytes 12582912 | tf_op jit(solution)/shard_map/all_to_all | solution.py:86
where the time goes:
time: 381 us; the launch traced here: 380 us
  blocking collectives  144 us (38%)
  waiting for transfers between devices  137 us (36%)
  local copies, waits for them, and re-layouts  48.8 us (13%)
  matrix products  23.1 us (6%)
  other arithmetic  21.1 us (6%)
  starting transfers between devices  5.63 us (1%)
    all_to_all x1, blocking collectives, local(): lax.all_to_all(doubled, 'expert', split_axis=0, concat_axis=0, tiled=True)  144 us
    all_to_all x1, waiting for transfers between devices, local(): lax.all_to_all(partial_value.reshape(sources, items, width), 'expert', sp...  137 us
    dot_general x1, matrix products, local(): jnp.dot(active, w_down[0], preferred_element_type=jnp.float32)  12.8 us
    unnamed x25, local copies, waits for them, and re-layouts  11.7 us
    scatter x1, local copies, waits for them, and re-layouts, local(): jnp.zeros((experts * capacity, width), jnp.bfloat16).at[target]  11.6 us
  transfers between devices with their start and end apart: 1, of which 1 were waited for; matrix products, arithmetic and copies ran while one was open for 0% of the time, Pallas kernels for 0%

commit v1 on v0

v1 whole, which is shorter than its diff:
```python
import jax
import jax.numpy as jnp
from jax import lax
from jax.experimental import pallas as pl
from jax.experimental.pallas import tpu as pltpu
from jax.sharding import PartitionSpec as P

HEADS = 32
KV_HEADS = 4
HEAD_DIM = 128
BLOCK = 32
GROUPS = HEADS // KV_HEADS
F32 = jnp.float32
BF16 = jnp.bfloat16


def attention_kernel(
    lens_ref, q_ref, bk_ref, bv_ref, ck_ref, cv_ref, resid_ref, gain_ref, hidden_ref, normed_ref
):
    request = pl.program_id(0)
    kv = pl.program_id(1)
    prefix = ck_ref.shape[1]
    length = lens_ref[request]
    q = q_ref[...]
    rows = jnp.concatenate([q[:, g * HEAD_DIM : (g + 1) * HEAD_DIM] for g in range(GROUPS)], 0)
    contract = (((1,), (1,)), ((), ()))
    scale = HEAD_DIM ** (-0.5)
    cached = lax.dot_general(rows, ck_ref[0], contract, preferred_element_type=F32) * scale
    own = lax.dot_general(rows, bk_ref[...], contract, preferred_element_type=F32) * scale
    position = lax.broadcasted_iota(jnp.int32, (1, prefix), 1)
    cached = jnp.where(position < length, cached, F32(-1e30))
    top = jnp.maximum(jnp.max(cached, -1, keepdims=True), jnp.max(own, -1, keepdims=True))
    cached = jnp.exp(cached - top)
    own = jnp.exp(own - top)
    total = jnp.sum(cached, -1, keepdims=True) + jnp.sum(own, -1, keepdims=True)
    mixed = jnp.dot(cached.astype(BF16), cv_ref[0], preferred_element_type=F32)
    mixed += jnp.dot(own.astype(BF16), bv_ref[...], preferred_element_type=F32)
    mixed = (mixed / total).astype(BF16)
    wide = GROUPS * HEAD_DIM
    attended = jnp.concatenate([mixed[g * BLOCK : (g + 1) * BLOCK] for g in range(GROUPS)], 1)
    columns = pl.ds(pl.multiple_of(kv * wide, wide), wide)
    hidden_ref[:, columns] = (
        resid_ref[:, columns].astype(F32) + attended.astype(F32)
    ).astype(BF16)

    @pl.when(kv == KV_HEADS - 1)
    def _():
        hidden = hidden_ref[...].astype(F32)
        normed_ref[...] = (
            hidden
            * lax.rsqrt(jnp.mean(hidden * hidden, -1, keepdims=True) + 1e-06)
            * gain_ref[...]
        ).astype(BF16)


def attend(resid, queries, block_keys, block_values, cache_keys, cache_values, prefix_len, gain):
    requests, prefix, _ = cache_keys.shape
    width = resid.shape[1]
    wide = GROUPS * HEAD_DIM
    rows_kv = pl.BlockSpec((BLOCK, HEAD_DIM), lambda r, k, lens: (r, k))
    cached = pl.BlockSpec((1, prefix, HEAD_DIM), lambda r, k, lens: (r, 0, k))
    whole = pl.BlockSpec((BLOCK, width), lambda r, k, lens: (r, 0))
    return pl.pallas_call(
        attention_kernel,
        grid_spec=pltpu.PrefetchScalarGridSpec(
            num_scalar_prefetch=1,
            grid=(requests, KV_HEADS),
            in_specs=[
                pl.BlockSpec((BLOCK, wide), lambda r, k, lens: (r, k)),
                rows_kv,
                rows_kv,
                cached,
                cached,
                whole,
                pl.BlockSpec((1, width), lambda r, k, lens: (0, 0)),
            ],
            out_specs=[whole, whole],
        ),
        out_shape=[jax.ShapeDtypeStruct(resid.shape, BF16)] * 2,
        compiler_params=pltpu.CompilerParams(vmem_limit_bytes=48 << 20),
        name="attention",
    )(prefix_len, queries, block_keys, block_values, cache_keys, cache_values, resid, gain[None, :])


def ffn(rows, weights):
    total = None
    for gate, up, down in weights:
        gate_out = jnp.dot(rows, gate, preferred_element_type=F32)
        upward = jnp.dot(rows, up, preferred_element_type=F32)
        active = (jax.nn.silu(gate_out) * upward).astype(BF16)
        part = jnp.dot(active, down, preferred_element_type=F32)
        total = part if total is None else total + part
    return total


def route_table(expert_ids, route_weights, experts):
    onehot = (expert_ids[:, :, None] == jnp.arange(experts, dtype=jnp.int32)).astype(F32)
    weight = jnp.sum(onehot * route_weights[:, :, None], 1)
    return jnp.concatenate([weight, jnp.sum(onehot, 1)], 1)


def pick_rows(mask, capacity):
    tokens = mask.shape[-1]
    order = jnp.arange(tokens, dtype=jnp.int32)
    before = (order[:, None] < order[None, :]).astype(F32)
    rank = jnp.dot(mask, before, preferred_element_type=F32)
    slot = jnp.arange(capacity, dtype=jnp.int32).astype(F32)
    return (rank[:, None, :] == slot[None, :, None]).astype(F32) * mask[:, None, :]


def pairs(step, flip, valid):
    found = []
    for z in range(4):
        for y in range(2):
            for c in range(2):
                to = step(z)
                if valid(z) and 0 <= to < 4:
                    found.append((4 * z + 2 * y + c, 4 * to + 2 * (y ^ flip) + c))
    return found


def always(z):
    return True


def ends(z):
    return z in (0, 3)


def middle(z):
    return z in (1, 2)


def send(value, step, flip, valid):
    return lax.ppermute(value, "expert", pairs(step, flip, valid))


def stay(z):
    return z


def plus(z):
    return z + 1


def minus(z):
    return z - 1


def grid_moe(hidden, normed, expert_ids, route_weights, weights, topk):
    position = lax.axis_index("expert")
    z, y = position // 4, (position // 2) % 2
    experts = 8
    tokens, width = normed.shape
    capacity = 2 * ((3 * tokens * topk + 4 * experts - 1) // (4 * experts))
    groups = [[2 * chip + core for chip in range(8)] for core in range(2)]
    table = lax.all_gather(
        route_table(expert_ids, route_weights, experts), "expert", axis_index_groups=groups
    )
    near = jnp.where(z == 0, 1, z - 1)
    late = jnp.where(z == 0, 3, jnp.where(z == 3, 0, z + 1))
    sources = jnp.stack([z, near, z ^ 2, late])
    mine = jnp.take(table, 2 * sources + y, axis=0)
    theirs = jnp.take(table, 2 * sources + 1 - y, axis=0)
    here, across = 2 * z + y, 2 * z + 1 - y

    def column(values, index):
        return lax.dynamic_index_in_dim(values, index, 2, keepdims=False)

    picks = pick_rows(column(mine, experts + across), capacity).astype(BF16)
    own_weight = column(mine, here)
    arriving = pick_rows(column(theirs, experts + here), capacity)
    cross_weight = jnp.sum(arriving * column(theirs, here)[:, None, :], 2)

    def pick(slot, rows):
        return jnp.dot(picks[slot], rows, preferred_element_type=F32).astype(BF16)

    def place(slot, rows):
        return jnp.dot(picks[slot].T, rows, preferred_element_type=F32)

    is_end = (z == 0) | (z == 3)
    up1 = send(normed, plus, 0, always)
    down1 = send(normed, minus, 0, always)
    cross0 = send(pick(0, normed), stay, 1, always)
    up2 = send(up1, plus, 0, lambda z: z >= 1)
    down2 = send(down1, minus, 0, lambda z: z <= 2)
    row_near = jnp.where(z == 0, down1, up1)
    cross_near = send(pick(1, row_near), stay, 1, always)
    cross_mid = send(pick(3, down1), stay, 1, middle)
    row_two = jnp.where(z >= 2, up2, down2)
    far = lax.ppermute(row_two, "expert", pairs(lambda z: {1: 0, 2: 3}.get(z, -1), 0, middle))
    cross_two = send(pick(2, row_two), stay, 1, always)
    cross_end = send(pick(3, far), stay, 1, ends)
    row_late = jnp.where(is_end, far, down1)
    cross_late = jnp.where(is_end, cross_end, cross_mid)

    rows = jnp.concatenate(
        [normed, row_near, row_two, row_late, cross0, cross_near, cross_two, cross_late], 0
    )
    scale = jnp.concatenate([own_weight.reshape(-1), cross_weight.reshape(-1)])
    out = (ffn(rows, weights) * scale[:, None]).astype(BF16)
    mine_out = [out[i * tokens : (i + 1) * tokens].astype(F32) for i in range(4)]
    base = 4 * tokens
    cross_out = [out[base + i * capacity : base + (i + 1) * capacity] for i in range(4)]

    back_end = send(cross_out[3], stay, 1, ends)
    back_two = send(cross_out[2], stay, 1, always)
    sum_far = mine_out[3] + place(3, back_end)
    got_far = lax.ppermute(
        sum_far.astype(BF16), "expert", pairs(lambda z: {0: 1, 3: 2}.get(z, -1), 0, ends)
    )
    sum_two = (mine_out[2] + place(2, back_two) + got_far.astype(F32)).astype(BF16)
    got_down = send(sum_two, minus, 0, lambda z: z >= 2)
    got_up = send(sum_two, plus, 0, lambda z: z <= 1)
    back_near = send(cross_out[1], stay, 1, always)
    back_mid = send(cross_out[3], stay, 1, middle)
    sum_near = (mine_out[1] + place(1, back_near) + got_down.astype(F32)).astype(BF16)
    sum_next = (mine_out[3] + place(3, back_mid) + got_up.astype(F32)).astype(BF16)
    last_up = send(jnp.where(z == 0, sum_near, sum_next), plus, 0, always)
    last_down = send(sum_near, minus, 0, always)
    back0 = send(cross_out[0], stay, 1, always)
    return (
        hidden.astype(F32)
        + mine_out[0]
        + place(0, back0)
        + last_up.astype(F32)
        + last_down.astype(F32)
    ).astype(BF16)


def gathered_moe(hidden, normed, expert_ids, route_weights, weights, topk):
    devices = lax.axis_size("expert")
    position = lax.axis_index("expert")
    chips = devices // 2
    groups = [[2 * chip + core for chip in range(chips)] for core in range(2)]
    table = lax.all_gather(
        route_table(expert_ids, route_weights, chips),
        "expert",
        tiled=True,
        axis_index_groups=groups,
    )
    rows = lax.all_gather(normed, "expert", tiled=True, axis_index_groups=groups)
    scale = lax.dynamic_index_in_dim(table, position // 2, 1)
    out = (ffn(rows, weights) * scale).astype(BF16)
    mixture = lax.psum_scatter(
        out, "expert", scatter_dimension=0, tiled=True, axis_index_groups=groups
    )
    return (hidden.astype(F32) + mixture.astype(F32)).astype(BF16)


def local(
    resid,
    queries,
    block_keys,
    block_values,
    cache_keys,
    cache_values,
    prefix_len,
    norm_gain,
    expert_ids,
    route_weights,
    w_gate,
    w_up,
    w_down,
):
    devices = lax.axis_size("expert")
    swap = [(device, device ^ 1) for device in range(devices)]
    held = (w_gate[0], w_up[0], w_down[0])
    other = tuple(lax.ppermute(part, "expert", swap) for part in held)
    hidden, normed = attend(
        resid,
        queries,
        block_keys,
        block_values,
        cache_keys,
        cache_values,
        prefix_len,
        norm_gain,
    )
    moe = grid_moe if devices == 16 else gathered_moe
    return moe(
        hidden, normed, expert_ids, route_weights, (held, other), expert_ids.shape[1]
    )


def solution(mesh):
    rows = P(("group", "expert"), None)
    cube = P(("group", "expert"), None, None)
    slices = P("expert", None, None)
    placed = (
        rows,
        rows,
        rows,
        rows,
        cube,
        cube,
        P(("group", "expert")),
        P(),
        rows,
        rows,
        slices,
        slices,
        slices,
    )
    return jax.shard_map(local, mesh=mesh, in_specs=placed, out_specs=rows, check_vma=False)
```

time: 381 us -> 222 us (0.58)
  the two profiles are of different devices: /device:TPU:13 before, /device:TPU:0 now
where the time goes in v1:
time: 222 us; the launch traced here: 221 us
  waiting for transfers between devices  82.7 us (37%)
  starting transfers between devices  43.7 us (20%)
  blocking collectives  40.5 us (18%)
  matrix products  30.6 us (14%)
  local copies, waits for them, and re-layouts  11.7 us (5%)
  Pallas kernels  9.19 us (4%)
  other arithmetic  2.47 us (1%)
    ppermute x18, waiting for transfers between devices, send(): return lax.ppermute(value, 'expert', pairs(step, flip, valid))  68.3 us
    all_gather x1, blocking collectives, grid_moe(): lax.all_gather(route_table(expert_ids, route_weights, experts), 'expert',...  40.5 us
    ppermute x18, starting transfers between devices, send(): return lax.ppermute(value, 'expert', pairs(step, flip, valid))  40.4 us
    dot_general x2, matrix products, ffn(): part = jnp.dot(active, down, preferred_element_type=F32)  21.4 us
    ppermute x1, waiting for transfers between devices, grid_moe(): lax.ppermute(row_two, 'expert', pairs(lambda z: {1: 0, 2: 3}.get(z, -1),...  12.9 us
    pallas_call x1, Pallas kernels, attend(): pl.pallas_call(attention_kernel, grid_spec=pltpu.PrefetchScalarGridSpec(n...  9.19 us
    unnamed x28, local copies, waits for them, and re-layouts  8.79 us
    dot_general x2, matrix products, ffn(): gate_out = jnp.dot(rows, gate, preferred_element_type=F32)  4.93 us
  transfers between devices with their start and end apart: 23, of which 12 were waited for; matrix products, arithmetic and copies ran while one was open for 10% of the time, Pallas kernels for 0%

profile of v1, /device:TPU:0, one launch (start us, length us, event | category | flops | bytes accessed | tf_op | source)
XLA Modules:
  0.0 221.4 jit_solution(17189505880524504957)
XLA Ops:
  0.0 1.6 copy-done
  1.6 1.0 copy-done.1
  2.6 1.0 copy-done.2
  3.7 0.8 copy-done.3
  4.5 0.8 copy-done.4
  5.4 0.7 copy-done.5
  6.1 0.7 copy-done.6
  6.7 9.2 %attention.1 = (bf16[64,4096]{1,0:T(8,128)(2,1)S(1)}, bf16[64,4096]{1,0:T(8,128)(2,1)S(1)}) custom-call(s32[2]{0:T(128)S(1)} %copy-done.6, bf16[64,4096]{1,0:T(8,128)(2,1)S(1)} %copy-done.1, bf16[64,512]{1,0:T(8,128)(2,1)S(1)} %copy-done.3, bf16[64,512]{1,0:T(8,128)(2,1)S(1)} %copy-done.4, bf16[2,1024,512]{2,1,0:T(8,128)(2,1)S(1)} %copy-done, ...), custom_call_target="tpu_custom_call" | custom-call | tf_op jit(solution)/shard_map/attention/pallas_call | solution.py:63
  15.9 5.0 %collective-permute-start.1 = (bf16[64,4096]{1,0:T(8,128)(2,1)S(1)}, bf16[64,4096]{1,0:T(8,128)(2,1)S(1)}, u32[]{:S(2)}, u32[]{:S(2)}) collective-permute-start(bf16[64,4096]{1,0:T(8,128)(2,1)S(1)} %get-tuple-element.9), channel_id=1, source_target_pairs={{0,4},{1,5},{2,6},{3,7},{4,8},{5,9},{6,10},{7,11},{8,12},{9,13},{1... | collective-permute-start | bytes 1572872 | tf_op jit(solution)/shard_map/ppermute | solution.py:135
  20.9 1.3 collective-permute-start
  22.4 40.5 %all-gather.1 = f32[8,64,16]{1,2,0:T(8,128)S(1)} all-gather(f32[1,64,16]{1,2,0:T(8,128)S(1)} %maximum_bitcast_fusion), channel_id=2, replica_groups={{0,2,4,6,8,10,12,14},{1,3,5,7,9,11,13,15},{16,18,20,22,24,26,28,30},{17..., dimensions={0}, use_global_device_ids=true | all-gather | bytes 36864 | tf_op jit(solution)/shard_map/all_gather | solution.py:157
  62.9 0.5 gather_fusion
  65.9 0.7 collective-permute-start.2
  66.6 1.3 collective-permute-start.3
  68.2 14.2 %collective-permute-done.3 = bf16[64,4096]{1,0:T(8,128)(2,1)S(1)} collective-permute-done((bf16[64,4096]{1,0:T(8,128)(2,1)S(1)}, bf16[64,4096]{1,0:T(8,128)(2,1)S(1)}, u32[]{:S(2)}, u32[]{:S(2)}) %collective-permute-start.3) | collective-permute-done | bytes 524320 | tf_op jit(solution)/shard_map/ppermute | solution.py:135
  82.5 1.3 collective-permute-start.4
  84.6 12.9 %collective-permute-done.4 = bf16[64,4096]{1,0:T(8,128)(2,1)S(1)} collective-permute-done((bf16[64,4096]{1,0:T(8,128)(2,1)S(1)}, bf16[64,4096]{1,0:T(8,128)(2,1)S(1)}, u32[]{:S(2)}, u32[]{:S(2)}) %collective-permute-start.4) | collective-permute-done | bytes 524320 | tf_op jit(solution)/shard_map/ppermute | solution.py:191
  97.5 1.8 collective-permute-start.6
  99.7 0.7 collective-permute-start.9
  100.4 6.4 %collective-permute-done.6 = bf16[48,4096]{1,0:T(8,128)(2,1)S(1)} collective-permute-done((bf16[48,4096]{1,0:T(8,128)(2,1)S(1)}, bf16[48,4096]{1,0:T(8,128)(2,1)S(1)}, u32[]{:S(2)}, u32[]{:S(2)}) %collective-permute-start.6) | collective-permute-done | bytes 393248 | tf_op jit(solution)/shard_map/ppermute | solution.py:135
  106.8 1.7 collective-permute-start.7
  108.6 6.7 %collective-permute-done.7 = bf16[48,4096]{1,0:T(8,128)(2,1)S(1)} collective-permute-done((bf16[48,4096]{1,0:T(8,128)(2,1)S(1)}, bf16[48,4096]{1,0:T(8,128)(2,1)S(1)}, u32[]{:S(2)}, u32[]{:S(2)}) %collective-permute-start.7) | collective-permute-done | bytes 393248 | tf_op jit(solution)/shard_map/ppermute | solution.py:135
  115.3 3.8 %collective-permute-start.8 = (bf16[48,4096]{1,0:T(8,128)(2,1)S(1)}, bf16[48,4096]{1,0:T(8,128)(2,1)S(1)}, u32[]{:S(2)}, u32[]{:S(2)}) collective-permute-start(bf16[48,4096]{1,0:T(8,128)(2,1)S(1)} %convolution_convert_fusion.1), channel_id=1, source_target_pairs={{0,2},{1,3},{2,0},{3,1},{12,14},{13,15},{14,12},{15,13},{16,18},{1... | collective-permute-start | bytes 1179656 | tf_op jit(solution)/shard_map/ppermute | solution.py:135
  119.1 5.8 %collective-permute-done.8 = bf16[48,4096]{1,0:T(8,128)(2,1)S(1)} collective-permute-done((bf16[48,4096]{1,0:T(8,128)(2,1)S(1)}, bf16[48,4096]{1,0:T(8,128)(2,1)S(1)}, u32[]{:S(2)}, u32[]{:S(2)}) %collective-permute-start.8) | collective-permute-done | bytes 393248 | tf_op jit(solution)/shard_map/ppermute | solution.py:135
  125.0 1.9 copy-done.8
  127.0 1.1 fusion.20
  128.1 10.2 %fusion.4 = f32[448,4096]{1,0:T(8,128)} fusion(f32[448,256]{1,0:T(8,128)S(1)} %fusion.20, bf16[1,256,4096]{2,1,0:T(8,128)(2,1)} %param.27, bf16[448,4096]{1,0:T(8,128)(2,1)} %copy-done.8, bf16[1,4096,256]{2,1,0:T(8,128)(2,1)} %param.26), kind=kOutput, calls=%fused_computation.23 | convolution fusion | flops 1879736320 | bytes 15663104 | tf_op jit(solution)/shard_map/dot_general | solution.py:91
  138.3 3.8 %fusion.27 = f32[448,256]{1,0:T(8,128)S(1)} fusion(bf16[448,4096]{1,0:T(8,128)(2,1)} %copy-done.8, bf16[4096,256]{1,0:T(8,128)(2,1)} %collective-permute-done.10), kind=kOutput, calls=%fused_computation.72 | convolution fusion | flops 939524096 | bytes 6225920 | tf_op jit(solution)/shard_map/dot_general | solution.py:88
  142.1 11.2 %multiply_convert_fusion = bf16[448,4096]{1,0:T(8,128)(2,1)} fusion(f32[448,4096]{1,0:T(8,128)} %fusion.4, bf16[256,4096]{1,0:T(8,128)(2,1)} %collective-permute-done.12, f32[448]{0:T(512)S(1)} %pad_maximum_fusion, f32[448,256]{1,0:T(8,128)S(1)} %fusion.27, bf16[448,4096]{1,0:T(8,128)(2,1)} %copy-done.8, bf16[4096,256]{1,0:T(8,128)(2,1)} %collective-permute-done.11), kind=kOutput, calls=%fused_computation.2 | convolution fusion | flops 1885241344 | bytes 19334912 | tf_op jit(solution)/shard_map/dot_general | solution.py:91
  153.3 1.6 fusion.24
  155.0 3.6 %collective-permute-start.16 = (bf16[48,4096]{1,0:T(8,128)(2,1)S(1)}, bf16[48,4096]{1,0:T(8,128)(2,1)S(1)}, u32[]{:S(2)}, u32[]{:S(2)}) collective-permute-start(bf16[48,4096]{1,0:T(8,128)(2,1)S(1)} %get-tuple-element.20), channel_id=1, source_target_pairs={{0,2},{1,3},{2,0},{3,1},{12,14},{13,15},{14,12},{15,13},{16,18},{1... | collective-permute-start | bytes 1179656 | tf_op jit(solution)/shard_map/ppermute | solution.py:135
  159.0 9.9 %collective-permute-done.16 = bf16[48,4096]{1,0:T(8,128)(2,1)S(1)} collective-permute-done((bf16[48,4096]{1,0:T(8,128)(2,1)S(1)}, bf16[48,4096]{1,0:T(8,128)(2,1)S(1)}, u32[]{:S(2)}, u32[]{:S(2)}) %collective-permute-start.16) | collective-permute-done | bytes 393248 | tf_op jit(solution)/shard_map/ppermute | solution.py:135
  168.9 1.4 fusion.2
  170.3 1.3 collective-permute-start.17
  171.6 1.7 collective-permute-start.14
  173.4 4.0 %collective-permute-done.15 = bf16[48,4096]{1,0:T(8,128)(2,1)S(1)} collective-permute-done((bf16[48,4096]{1,0:T(8,128)(2,1)S(1)}, bf16[48,4096]{1,0:T(8,128)(2,1)S(1)}, u32[]{:S(2)}, u32[]{:S(2)}) %collective-permute-start.15) | collective-permute-done | bytes 393248 | tf_op jit(solution)/shard_map/ppermute | solution.py:135
  177.7 1.5 collective-permute-done.17
  179.3 0.7 collective-permute-start.18
  180.0 0.7 collective-permute-start.19
  180.7 1.8 collective-permute-start.13
  182.5 1.8 collective-permute-done.14
  184.6 4.7 %collective-permute-start.20 = (bf16[64,4096]{1,0:T(8,128)(2,1)S(1)}, bf16[64,4096]{1,0:T(8,128)(2,1)S(1)}, u32[]{:S(2)}, u32[]{:S(2)}) collective-permute-start(bf16[64,4096]{1,0:T(8,128)(2,1)S(1)} %add_convert_fusion.2), channel_id=1, source_target_pairs={{0,4},{1,5},{2,6},{3,7},{4,8},{5,9},{6,10},{7,11},{16,20},{17,21},... | collective-permute-start | bytes 1572872 | tf_op jit(solution)/shard_map/ppermute | solution.py:135
  189.6 9.5 %collective-permute-done.20 = bf16[64,4096]{1,0:T(8,128)(2,1)S(1)} collective-permute-done((bf16[64,4096]{1,0:T(8,128)(2,1)S(1)}, bf16[64,4096]{1,0:T(8,128)(2,1)S(1)}, u32[]{:S(2)}, u32[]{:S(2)}) %collective-permute-start.20) | collective-permute-done | bytes 524320 | tf_op jit(solution)/shard_map/ppermute | solution.py:135
  199.5 9.2 %collective-permute-start.21 = (bf16[64,4096]{1,0:T(8,128)(2,1)S(1)}, bf16[64,4096]{1,0:T(8,128)(2,1)S(1)}, u32[]{:S(2)}, u32[]{:S(2)}) collective-permute-start(bf16[64,4096]{1,0:T(8,128)(2,1)S(1)} %fusion.3), channel_id=1, source_target_pairs={{0,4},{1,5},{2,6},{3,7},{4,8},{5,9},{6,10},{7,11},{8,12},{9,13},{1... | collective-permute-start | bytes 1572872 | tf_op jit(solution)/shard_map/ppermute | solution.py:135
  208.7 1.3 collective-permute-start.22
  210.4 5.0 %collective-permute-done.21 = bf16[64,4096]{1,0:T(8,128)(2,1)S(1)} collective-permute-done((bf16[64,4096]{1,0:T(8,128)(2,1)S(1)}, bf16[64,4096]{1,0:T(8,128)(2,1)S(1)}, u32[]{:S(2)}, u32[]{:S(2)}) %collective-permute-start.21) | collective-permute-done | bytes 524320 | tf_op jit(solution)/shard_map/ppermute | solution.py:135
  215.4 4.9 %collective-permute-done.22 = bf16[64,4096]{1,0:T(8,128)(2,1)S(1)} collective-permute-done((bf16[64,4096]{1,0:T(8,128)(2,1)S(1)}, bf16[64,4096]{1,0:T(8,128)(2,1)S(1)}, u32[]{:S(2)}, u32[]{:S(2)}) %collective-permute-start.22) | collective-permute-done | bytes 524320 | tf_op jit(solution)/shard_map/ppermute | solution.py:135
  220.2 1.1 add_convert_fusion
  (69 shorter events, 6.4 us)
Async XLA Ops:
  0.0 1.6 copy-start
  1.6 1.0 copy-start.1
  2.6 1.0 copy-start.2
  3.7 0.8 copy-start.3
  4.5 0.8 copy-start.4
  5.4 0.7 copy-start.5
  6.1 0.7 copy-start.6
  6.7 15.7 %copy-start.9 = (f32[64,4]{0,1:T(4,128)S(1)}, f32[64,4]{0,1:T(4,128)}, u32[]{:S(2)}) copy-start(f32[64,4]{0,1:T(4,128)} %param.24) | copy-start | bytes 3076
  6.7 15.7 %copy-start.10 = (s32[64,4]{0,1:T(4,128)S(1)}, s32[64,4]{0,1:T(4,128)}, u32[]{:S(2)}) copy-start(s32[64,4]{0,1:T(4,128)} %param.23) | copy-start | bytes 3076
  15.9 50.0 %collective-permute-start.1 = (bf16[64,4096]{1,0:T(8,128)(2,1)S(1)}, bf16[64,4096]{1,0:T(8,128)(2,1)S(1)}, u32[]{:S(2)}, u32[]{:S(2)}) collective-permute-start(bf16[64,4096]{1,0:T(8,128)(2,1)S(1)} %get-tuple-element.9), channel_id=1, source_target_pairs={{0,4},{1,5},{2,6},{3,7},{4,8},{5,9},{6,10},{7,11},{8,12},{9,13},{1... | collective-permute-start | bytes 1572872 | tf_op jit(solution)/shard_map/ppermute | solution.py:135
  20.9 45.7 %collective-permute-start = (bf16[64,4096]{1,0:T(8,128)(2,1)S(1)}, bf16[64,4096]{1,0:T(8,128)(2,1)S(1)}, u32[]{:S(2)}, u32[]{:S(2)}) collective-permute-start(bf16[64,4096]{1,0:T(8,128)(2,1)S(1)} %get-tuple-element.9), channel_id=1, source_target_pairs={{4,0},{5,1},{6,2},{7,3},{8,4},{9,5},{10,6},{11,7},{12,8},{13,9},{1... | collective-permute-start | bytes 1572872 | tf_op jit(solution)/shard_map/ppermute | solution.py:135
  64.1 35.6 %collective-permute-start.5 = (bf16[48,4096]{1,0:T(8,128)(2,1)S(1)}, bf16[48,4096]{1,0:T(8,128)(2,1)S(1)}, u32[]{:S(2)}, u32[]{:S(2)}) collective-permute-start(bf16[48,4096]{1,0:T(8,128)(2,1)S(1)} %convolution_convert_fusion.4), channel_id=1, source_target_pairs={{0,2},{1,3},{2,0},{3,1},{4,6},{5,7},{6,4},{7,5},{8,10},{9,11},{10,... | collective-permute-start | bytes 1179656 | tf_op jit(solution)/shard_map/ppermute | solution.py:135
  64.1 78.0 %collective-permute-start.12 = (bf16[256,4096]{1,0:T(8,128)(2,1)}, bf16[256,4096]{1,0:T(8,128)(2,1)}, u32[]{:S(2)}, u32[]{:S(2)}) collective-permute-start(bf16[256,4096]{1,0:T(8,128)(2,1)} %bitcast.60), channel_id=1, source_target_pairs={{0,1},{1,0},{2,3},{3,2},{4,5},{5,4},{6,7},{7,6},{8,9},{9,8},{10,11... | collective-permute-start | bytes 6291464 | tf_op jit(solution)/shard_map/ppermute | solution.py:269
  64.2 77.9 %collective-permute-start.11 = (bf16[4096,256]{1,0:T(8,128)(2,1)}, bf16[4096,256]{1,0:T(8,128)(2,1)}, u32[]{:S(2)}, u32[]{:S(2)}) collective-permute-start(bf16[4096,256]{1,0:T(8,128)(2,1)} %bitcast.61), channel_id=1, source_target_pairs={{0,1},{1,0},{2,3},{3,2},{4,5},{5,4},{6,7},{7,6},{8,9},{9,8},{10,11... | collective-permute-start | bytes 6291464 | tf_op jit(solution)/shard_map/ppermute | solution.py:269
  65.9 2.1 collective-permute-start.2
  66.6 15.8 %collective-permute-start.3 = (bf16[64,4096]{1,0:T(8,128)(2,1)S(1)}, bf16[64,4096]{1,0:T(8,128)(2,1)S(1)}, u32[]{:S(2)}, u32[]{:S(2)}) collective-permute-start(bf16[64,4096]{1,0:T(8,128)(2,1)S(1)} %collective-permute-done), channel_id=1, source_target_pairs={{4,0},{5,1},{6,2},{7,3},{8,4},{9,5},{10,6},{11,7},{20,16},{21,17},... | collective-permute-start | bytes 1572872 | tf_op jit(solution)/shard_map/ppermute | solution.py:135
  68.0 70.2 %collective-permute-start.10 = (bf16[4096,256]{1,0:T(8,128)(2,1)}, bf16[4096,256]{1,0:T(8,128)(2,1)}, u32[]{:S(2)}, u32[]{:S(2)}) collective-permute-start(bf16[4096,256]{1,0:T(8,128)(2,1)} %bitcast.67), channel_id=1, source_target_pairs={{0,1},{1,0},{2,3},{3,2},{4,5},{5,4},{6,7},{7,6},{8,9},{9,8},{10,11... | collective-permute-start | bytes 6291464 | tf_op jit(solution)/shard_map/ppermute | solution.py:269
  82.5 15.0 %collective-permute-start.4 = (bf16[64,4096]{1,0:T(8,128)(2,1)S(1)}, bf16[64,4096]{1,0:T(8,128)(2,1)S(1)}, u32[]{:S(2)}, u32[]{:S(2)}) collective-permute-start(bf16[64,4096]{1,0:T(8,128)(2,1)S(1)} %get-tuple-element.18), channel_id=1, source_target_pairs={{4,0},{5,1},{6,2},{7,3},{8,12},{9,13},{10,14},{11,15},{20,16},{21,... | collective-permute-start | bytes 1572872 | tf_op jit(solution)/shard_map/ppermute | solution.py:191
  84.3 42.6 %copy-start.11 = (bf16[1,4096,256]{2,1,0:T(8,128)(2,1)S(1)}, bf16[1,4096,256]{2,1,0:T(8,128)(2,1)}, u32[]{:S(2)}) copy-start(bf16[1,4096,256]{2,1,0:T(8,128)(2,1)} %param.25) | copy-start | bytes 6291460
  97.5 9.3 %collective-permute-start.6 = (bf16[48,4096]{1,0:T(8,128)(2,1)S(1)}, bf16[48,4096]{1,0:T(8,128)(2,1)S(1)}, u32[]{:S(2)}, u32[]{:S(2)}) collective-permute-start(bf16[48,4096]{1,0:T(8,128)(2,1)S(1)} %convolution_convert_fusion.3), channel_id=1, source_target_pairs={{0,2},{1,3},{2,0},{3,1},{4,6},{5,7},{6,4},{7,5},{8,10},{9,11},{10,... | collective-permute-start | bytes 1179656 | tf_op jit(solution)/shard_map/ppermute | solution.py:135
  99.7 19.4 %collective-permute-start.9 = (bf16[48,4096]{1,0:T(8,128)(2,1)S(1)}, bf16[48,4096]{1,0:T(8,128)(2,1)S(1)}, u32[]{:S(2)}, u32[]{:S(2)}) collective-permute-start(bf16[48,4096]{1,0:T(8,128)(2,1)S(1)} %convolution_convert_fusion), channel_id=1, source_target_pairs={{4,6},{5,7},{6,4},{7,5},{8,10},{9,11},{10,8},{11,9},{20,22},{21,23... | collective-permute-start | bytes 1179656 | tf_op jit(solution)/shard_map/ppermute | solution.py:135
  106.8 8.4 %collective-permute-start.7 = (bf16[48,4096]{1,0:T(8,128)(2,1)S(1)}, bf16[48,4096]{1,0:T(8,128)(2,1)S(1)}, u32[]{:S(2)}, u32[]{:S(2)}) collective-permute-start(bf16[48,4096]{1,0:T(8,128)(2,1)S(1)} %convolution_convert_fusion.2), channel_id=1, source_target_pairs={{0,2},{1,3},{2,0},{3,1},{4,6},{5,7},{6,4},{7,5},{8,10},{9,11},{10,... | collective-permute-start | bytes 1179656 | tf_op jit(solution)/shard_map/ppermute | solution.py:135
  115.3 9.7 %collective-permute-start.8 = (bf16[48,4096]{1,0:T(8,128)(2,1)S(1)}, bf16[48,4096]{1,0:T(8,128)(2,1)S(1)}, u32[]{:S(2)}, u32[]{:S(2)}) collective-permute-start(bf16[48,4096]{1,0:T(8,128)(2,1)S(1)} %convolution_convert_fusion.1), channel_id=1, source_target_pairs={{0,2},{1,3},{2,0},{3,1},{12,14},{13,15},{14,12},{15,13},{16,18},{1... | collective-permute-start | bytes 1179656 | tf_op jit(solution)/shard_map/ppermute | solution.py:135
  125.0 1.9 copy-start.8
  153.3 25.8 %copy-start.7 = (bf16[448,4096]{1,0:T(8,128)(2,1)S(1)}, bf16[448,4096]{1,0:T(8,128)(2,1)}, u32[]{:S(2)}) copy-start(bf16[448,4096]{1,0:T(8,128)(2,1)} %multiply_convert_fusion) | copy-start | bytes 11010052
  155.0 13.9 %collective-permute-start.16 = (bf16[48,4096]{1,0:T(8,128)(2,1)S(1)}, bf16[48,4096]{1,0:T(8,128)(2,1)S(1)}, u32[]{:S(2)}, u32[]{:S(2)}) collective-permute-start(bf16[48,4096]{1,0:T(8,128)(2,1)S(1)} %get-tuple-element.20), channel_id=1, source_target_pairs={{0,2},{1,3},{2,0},{3,1},{12,14},{13,15},{14,12},{15,13},{16,18},{1... | collective-permute-start | bytes 1179656 | tf_op jit(solution)/shard_map/ppermute | solution.py:135
  158.6 18.8 %collective-permute-start.15 = (bf16[48,4096]{1,0:T(8,128)(2,1)S(1)}, bf16[48,4096]{1,0:T(8,128)(2,1)S(1)}, u32[]{:S(2)}, u32[]{:S(2)}) collective-permute-start(bf16[48,4096]{1,0:T(8,128)(2,1)S(1)} %get-tuple-element.21), channel_id=1, source_target_pairs={{0,2},{1,3},{2,0},{3,1},{4,6},{5,7},{6,4},{7,5},{8,10},{9,11},{10,... | collective-permute-start | bytes 1179656 | tf_op jit(solution)/shard_map/ppermute | solution.py:135
  170.3 8.8 %collective-permute-start.17 = (bf16[64,4096]{1,0:T(8,128)(2,1)S(1)}, bf16[64,4096]{1,0:T(8,128)(2,1)S(1)}, u32[]{:S(2)}, u32[]{:S(2)}) collective-permute-start(bf16[64,4096]{1,0:T(8,128)(2,1)S(1)} %fusion.2), channel_id=1, source_target_pairs={{0,4},{1,5},{2,6},{3,7},{12,8},{13,9},{14,10},{15,11},{16,20},{17,... | collective-permute-start | bytes 1572872 | tf_op jit(solution)/shard_map/ppermute | solution.py:209
  171.6 12.7 %collective-permute-start.14 = (bf16[48,4096]{1,0:T(8,128)(2,1)S(1)}, bf16[48,4096]{1,0:T(8,128)(2,1)S(1)}, u32[]{:S(2)}, u32[]{:S(2)}) collective-permute-start(bf16[48,4096]{1,0:T(8,128)(2,1)S(1)} %get-tuple-element.22), channel_id=1, source_target_pairs={{0,2},{1,3},{2,0},{3,1},{4,6},{5,7},{6,4},{7,5},{8,10},{9,11},{10,... | collective-permute-start | bytes 1179656 | tf_op jit(solution)/shard_map/ppermute | solution.py:135
  179.3 10.1 %collective-permute-start.18 = (bf16[64,4096]{1,0:T(8,128)(2,1)S(1)}, bf16[64,4096]{1,0:T(8,128)(2,1)S(1)}, u32[]{:S(2)}, u32[]{:S(2)}) collective-permute-start(bf16[64,4096]{1,0:T(8,128)(2,1)S(1)} %add_convert_fusion.2), channel_id=1, source_target_pairs={{8,4},{9,5},{10,6},{11,7},{12,8},{13,9},{14,10},{15,11},{24,20},{2... | collective-permute-start | bytes 1572872 | tf_op jit(solution)/shard_map/ppermute | solution.py:135
  180.0 9.5 %collective-permute-start.19 = (bf16[48,4096]{1,0:T(8,128)(2,1)S(1)}, bf16[48,4096]{1,0:T(8,128)(2,1)S(1)}, u32[]{:S(2)}, u32[]{:S(2)}) collective-permute-start(bf16[48,4096]{1,0:T(8,128)(2,1)S(1)} %get-tuple-element.20), channel_id=1, source_target_pairs={{4,6},{5,7},{6,4},{7,5},{8,10},{9,11},{10,8},{11,9},{20,22},{21,23... | collective-permute-start | bytes 1179656 | tf_op jit(solution)/shard_map/ppermute | solution.py:135
  180.7 29.3 %collective-permute-start.13 = (bf16[48,4096]{1,0:T(8,128)(2,1)S(1)}, bf16[48,4096]{1,0:T(8,128)(2,1)S(1)}, u32[]{:S(2)}, u32[]{:S(2)}) collective-permute-start(bf16[48,4096]{1,0:T(8,128)(2,1)S(1)} %get-tuple-element.19), channel_id=1, source_target_pairs={{0,2},{1,3},{2,0},{3,1},{4,6},{5,7},{6,4},{7,5},{8,10},{9,11},{10,... | collective-permute-start | bytes 1179656 | tf_op jit(solution)/shard_map/ppermute | solution.py:135
  184.6 14.4 %collective-permute-start.20 = (bf16[64,4096]{1,0:T(8,128)(2,1)S(1)}, bf16[64,4096]{1,0:T(8,128)(2,1)S(1)}, u32[]{:S(2)}, u32[]{:S(2)}) collective-permute-start(bf16[64,4096]{1,0:T(8,128)(2,1)S(1)} %add_convert_fusion.2), channel_id=1, source_target_pairs={{0,4},{1,5},{2,6},{3,7},{4,8},{5,9},{6,10},{7,11},{16,20},{17,21},... | collective-permute-start | bytes 1572872 | tf_op jit(solution)/shard_map/ppermute | solution.py:135
  199.5 15.9 %collective-permute-start.21 = (bf16[64,4096]{1,0:T(8,128)(2,1)S(1)}, bf16[64,4096]{1,0:T(8,128)(2,1)S(1)}, u32[]{:S(2)}, u32[]{:S(2)}) collective-permute-start(bf16[64,4096]{1,0:T(8,128)(2,1)S(1)} %fusion.3), channel_id=1, source_target_pairs={{0,4},{1,5},{2,6},{3,7},{4,8},{5,9},{6,10},{7,11},{8,12},{9,13},{1... | collective-permute-start | bytes 1572872 | tf_op jit(solution)/shard_map/ppermute | solution.py:135
  208.7 11.5 %collective-permute-start.22 = (bf16[64,4096]{1,0:T(8,128)(2,1)S(1)}, bf16[64,4096]{1,0:T(8,128)(2,1)S(1)}, u32[]{:S(2)}, u32[]{:S(2)}) collective-permute-start(bf16[64,4096]{1,0:T(8,128)(2,1)S(1)} %add_convert_fusion.1), channel_id=1, source_target_pairs={{4,0},{5,1},{6,2},{7,3},{8,4},{9,5},{10,6},{11,7},{12,8},{13,9},{1... | collective-permute-start | bytes 1572872 | tf_op jit(solution)/shard_map/ppermute | solution.py:135
